TPU v7x, 256 devices: a whole 4x4x8 slice. The times are simulated.
256 devices in a mesh: grp: 8 (over z_lo, core), nbr: 32 (over z_hi, y, x).
Axes of the slice: x: 4, y: 4, z: 8 (z_hi: 2, z_lo: 4; z = z_hi * 4 + z_lo), core: 2. Of those that a mesh axis runs over, the one named last changes fastest.
Arguments:
- tokens: bfloat16 [32, 448, 4096], P('nbr'), may hold values from -6 to 6
- encoded: bfloat16 [64, 128, 4096], P('nbr'), may hold values from -6 to 6
- neighbour_ids: int32 [32, 7, 2], P('nbr'), may hold values from 0 to 63, as said below
- w_query: bfloat16 [4096, 2048], P('nbr', 'grp'), may hold values from -0.09375 to 0.09375
- w_key: bfloat16 [4096, 2048], P('nbr', 'grp'), may hold values from -0.09375 to 0.09375
- w_value: bfloat16 [4096, 2048], P('nbr', 'grp'), may hold values from -0.09375 to 0.09375
- w_out: bfloat16 [2048, 4096], P('grp', 'nbr'), may hold values from -0.125 to 0.125
- d_out: bfloat16 [32, 448, 4096], P('nbr'), may hold values from -6 to 6
Outputs:
- attended: bfloat16 [32, 448, 4096], P('nbr', None, 'grp')
- d_tokens: bfloat16 [32, 448, 4096], P('nbr', None, 'grp')
- grad_query: float32 [4096, 2048], P('nbr', 'grp')
- grad_key: float32 [4096, 2048], P('nbr', 'grp')
- grad_value: float32 [4096, 2048], P('nbr', 'grp')
- grad_out: float32 [2048, 4096], P('grp', 'nbr')
Inputs may be any that keep to these rules, and one draw needn't show every extreme that they name: `neighbour_ids`: within one sequence the 14 ids lie in distinct blocks of 2 consecutive entries (id // 2 differs between any two of them), and one such block is named by every sequence.
All inputs are finite; a program needn't handle non-finite values.
Results may differ from a plain program's by a relative error of at most 0.03.
Values may be sent and summed in bfloat16 or wider, within the bound.
No kernel may reach another device: no remote copies, remote signals or barrier semaphores. Data moves between devices by JAX's collectives and lax.ppermute only.
A program may use at most 128 MiB of HBM per device.

v0:
```python
import math

import jax
import jax.numpy as jnp
from jax import lax
from jax.sharding import PartitionSpec as P

HS = 128
CH = 64
NEIGH = 2
RLEN = 128


def shift_in(rows, span_len):
    filler = jnp.zeros((span_len - 1,) + rows.shape[1:], rows.dtype)
    return jnp.concatenate([rows[span_len - 1 :], filler], 0)


def shift_out(rows, span_len):
    filler = jnp.zeros((span_len - 1,) + rows.shape[1:], rows.dtype)
    return jnp.concatenate([filler, rows[: rows.shape[0] - span_len + 1]], 0)


def on_device(tokens, encoded, neighbour_ids, w_query, w_key, w_value, w_out, d_out):
    contract_rows = (((0,), (0,)), ((), ()))
    contract_cols = (((1,), (1,)), ((), ()))
    wq_group, wk_group, wv_group, wo_group = (
        lax.all_gather(w_query, "nbr", axis=0, tiled=True),
        lax.all_gather(w_key, "nbr", axis=0, tiled=True),
        lax.all_gather(w_value, "nbr", axis=0, tiled=True),
        lax.all_gather(w_out, "nbr", axis=1, tiled=True),
    )
    head_cols = wq_group.shape[1]
    group_heads = head_cols // HS
    score_scale = 1.0 / math.sqrt(HS)
    peers = lax.axis_size("nbr")
    entry_count = encoded.shape[0]
    rows_in = tokens[0]
    upstream = d_out[0]
    tok_count = rows_in.shape[0]
    span_count = tok_count // CH
    wanted = neighbour_ids[0].reshape(-1)
    owner_of = wanted // entry_count
    in_block = wanted % entry_count
    owner_match = owner_of[None, :] == jnp.arange(peers, dtype=jnp.int32)[:, None]
    asking = jnp.sum(jnp.where(owner_match, in_block[None, :] + 1, 0), axis=1) - 1
    asked_for = lax.all_to_all(asking[:, None], "nbr", split_axis=0, concat_axis=0, tiled=True)[
        :, 0
    ]
    enc_flat = encoded.reshape(entry_count * RLEN, encoded.shape[2])
    wkv_group = jnp.concatenate([wk_group, wv_group], 1)
    kv_local = jnp.dot(enc_flat, wkv_group, preferred_element_type=jnp.float32).astype(jnp.bfloat16)
    kv_local = kv_local.reshape(entry_count, RLEN, 2 * head_cols)
    answers = jnp.where(
        (asked_for >= 0)[:, None, None],
        kv_local[jnp.clip(asked_for, 0)],
        jnp.zeros((), jnp.bfloat16),
    )
    delivered = lax.all_to_all(answers, "nbr", split_axis=0, concat_axis=0, tiled=True)
    fetched = delivered[owner_of]
    fetched = fetched.reshape(span_count, NEIGH * RLEN, 2 * head_cols)
    key_rows = fetched[:, :, :head_cols].reshape(span_count, NEIGH * RLEN, group_heads, HS)
    value_rows = fetched[:, :, head_cols:].reshape(span_count, NEIGH * RLEN, group_heads, HS)
    query = jnp.dot(rows_in, wq_group, preferred_element_type=jnp.float32).astype(jnp.bfloat16)
    query_sh = shift_in(query, CH).reshape(span_count, CH, group_heads, HS)
    scores = (
        jnp.einsum("cqhe,ckhe->chqk", query_sh, key_rows, preferred_element_type=jnp.float32)
        * score_scale
    )
    raised = jnp.exp(scores)
    attn_probs = raised / jnp.sum(raised, -1, keepdims=True)
    probs_low = attn_probs.astype(jnp.bfloat16)
    context_sh = jnp.einsum(
        "chqk,ckhe->cqhe", probs_low, value_rows, preferred_element_type=jnp.float32
    )
    context = shift_out(context_sh.astype(jnp.bfloat16).reshape(tok_count, head_cols), CH)
    out_term = jnp.dot(context, wo_group, preferred_element_type=jnp.float32)
    attended = lax.psum_scatter(
        out_term.astype(jnp.bfloat16), "grp", scatter_dimension=1, tiled=True
    )
    d_context = lax.dot_general(
        upstream, wo_group, contract_cols, preferred_element_type=jnp.float32
    ).astype(jnp.bfloat16)
    d_ctx_sh = shift_in(d_context, CH).reshape(span_count, CH, group_heads, HS)
    d_probs = jnp.einsum(
        "cqhe,ckhe->chqk", d_ctx_sh, value_rows, preferred_element_type=jnp.float32
    )
    row_dot = jnp.sum(attn_probs * d_probs, -1, keepdims=True)
    d_scores = (attn_probs * (d_probs - row_dot)).astype(jnp.bfloat16)
    grad_query_sh = (
        jnp.einsum("chqk,ckhe->cqhe", d_scores, key_rows, preferred_element_type=jnp.float32)
        * score_scale
    )
    grad_keys = (
        jnp.einsum("chqk,cqhe->ckhe", d_scores, query_sh, preferred_element_type=jnp.float32)
        * score_scale
    )
    grad_values = jnp.einsum(
        "chqk,cqhe->ckhe", probs_low, d_ctx_sh, preferred_element_type=jnp.float32
    )
    grad_used = jnp.concatenate(
        [
            grad_keys.astype(jnp.bfloat16).reshape(span_count, NEIGH * RLEN, head_cols),
            grad_values.astype(jnp.bfloat16).reshape(span_count, NEIGH * RLEN, head_cols),
        ],
        -1,
    )
    grad_used = grad_used.reshape(span_count * NEIGH, RLEN, 2 * head_cols)
    outgoing = jnp.einsum(
        "om,mrp->orp",
        owner_match.astype(jnp.bfloat16),
        grad_used,
        preferred_element_type=jnp.float32,
    ).astype(jnp.bfloat16)
    incoming = lax.all_to_all(outgoing, "nbr", split_axis=0, concat_axis=0, tiled=True)
    entry_match = (asked_for[:, None] == jnp.arange(entry_count, dtype=jnp.int32)[None, :]).astype(
        jnp.bfloat16
    )
    entry_grads = jnp.einsum(
        "se,srp->erp", entry_match, incoming, preferred_element_type=jnp.float32
    ).astype(jnp.bfloat16)
    entry_grads = entry_grads.reshape(entry_count * RLEN, 2 * head_cols)
    grad_query_rows = shift_out(
        grad_query_sh.astype(jnp.bfloat16).reshape(tok_count, head_cols), CH
    )
    dx_term = lax.dot_general(
        grad_query_rows, wq_group, contract_cols, preferred_element_type=jnp.float32
    )
    d_tokens = lax.psum_scatter(
        dx_term.astype(jnp.bfloat16), "grp", scatter_dimension=1, tiled=True
    )
    from_tokens = lax.dot_general(
        rows_in, grad_query_rows, contract_rows, preferred_element_type=jnp.float32
    )
    from_entries = lax.dot_general(
        enc_flat, entry_grads, contract_rows, preferred_element_type=jnp.float32
    )
    stacked = lax.psum_scatter(
        jnp.concatenate(
            [
                jnp.concatenate([from_tokens, from_entries], 1),
                lax.dot_general(
                    upstream, context, contract_rows, preferred_element_type=jnp.float32
                ),
            ],
            1,
        ).astype(jnp.bfloat16),
        "nbr",
        scatter_dimension=0,
        tiled=True,
    ).astype(jnp.float32)
    late_in = stacked[:, : 3 * head_cols]
    grad_out_rows = stacked[:, 3 * head_cols :]
    grad_query = late_in[:, :head_cols]
    grad_key = late_in[:, head_cols : 2 * head_cols]
    grad_value = late_in[:, 2 * head_cols :]
    grad_out = grad_out_rows.T
    return (attended[None], d_tokens[None], grad_query, grad_key, grad_value, grad_out)


def solution(mesh):
    in_specs = (
        P("nbr", None, None),
        P("nbr", None, None),
        P("nbr", None, None),
        P("nbr", "grp"),
        P("nbr", "grp"),
        P("nbr", "grp"),
        P("grp", "nbr"),
        P("nbr", None, None),
    )
    out_specs = (
        P("nbr", None, "grp"),
        P("nbr", None, "grp"),
        P("nbr", "grp"),
        P("nbr", "grp"),
        P("nbr", "grp"),
        P("grp", "nbr"),
    )
    return jax.shard_map(
        on_device, mesh=mesh, in_specs=in_specs, out_specs=out_specs, check_vma=False
    )
```

profile of v0, /device:TPU:16, one launch (start us, length us, event | category | flops | bytes accessed | tf_op | source)
XLA Modules:
  0.0 1012.9 jit_solution(14342262496100488004)
XLA Ops:
  10.3 14.0 %all-to-all-start = ((s32[32,1,1]{2,1,0:T(1,128)}), s32[32,1,1]{2,1,0:T(1,128)S(1)}, u32[]{:S(2)}, u32[]{:S(2)}) async-start(s32[32,1,1]{2,1,0:T(1,128)} %copy.88), calls=%async_computation | async-start | bytes 32768 | tf_op jit(solution)/shard_map/all_to_all | solution.py:47
  25.1 9.3 all-to-all-done
  36.3 68.3 %all-gather.5.cloned.1.call-done = bf16[4096,256]{1,0:T(8,128)(2,1)} async-done(((bf16[128,256]{1,0:T(8,128)(2,1)}), bf16[4096,256]{1,0:T(8,128)(2,1)}) %all-gather.5.cloned.1.call-update) | async-done | bytes 2097168 | tf_op jit(solution)/shard_map/all_gather | solution.py:29
  104.7 89.2 %all-gather.7.cloned.1.call-done = bf16[4096,256]{1,0:T(8,128)(2,1)} async-done(((bf16[128,256]{1,0:T(8,128)(2,1)}), bf16[4096,256]{1,0:T(8,128)(2,1)}) %all-gather.7.cloned.1.call-update) | async-done | bytes 2097168 | tf_op jit(solution)/shard_map/all_gather | solution.py:30
  193.9 3.5 fusion.21
  197.3 2.8 gather_fusion
  200.1 4.5 broadcast_select_fusion
  204.6 6.6 all-to-all-start.1
  211.9 156.6 %all-gather.11.cloned.1.call-done = bf16[256,4096]{1,0:T(8,128)(2,1)} async-done(((bf16[256,128]{1,0:T(8,128)(2,1)}), bf16[256,4096]{1,0:T(8,128)(2,1)}) %all-gather.11.cloned.1.call-update) | async-done | bytes 2097168 | tf_op jit(solution)/shard_map/all_gather | solution.py:31
  368.5 3.9 fusion.10
  372.5 85.9 %all-gather.9.cloned.1.call-done = bf16[4096,256]{1,0:T(8,128)(2,1)} async-done(((bf16[128,256]{1,0:T(8,128)(2,1)}), bf16[4096,256]{1,0:T(8,128)(2,1)}) %all-gather.9.cloned.1.call-update) | async-done | bytes 2097168 | tf_op jit(solution)/shard_map/all_gather | solution.py:28
  458.4 3.8 fusion.13
  462.4 4.2 gather_fusion.1
  466.6 2.8 fusion.62
  472.2 3.0 fusion.19
  475.2 3.6 copy.103
  478.8 3.4 concatenate.33
  492.0 3.6 copy.101
  495.6 3.4 concatenate.32
  503.3 4.4 copy.106
  507.6 6.6 all-to-all-start.2
  514.5 2.9 fusion.28
  519.6 2.7 fusion.2
  524.9 50.2 %all-to-all-done.2 = bf16[32,128,512]{2,1,0:T(8,128)(2,1)} async-done(((bf16[32,128,512]{2,1,0:T(8,128)(2,1)}), bf16[32,128,512]{2,1,0:T(8,128)(2,1)}, u32[]{:S(2)}, u32[]{:S(2)}) %all-to-all-start.2) | async-done | bytes 4194336 | tf_op jit(solution)/shard_map/all_to_all | solution.py:115
  575.1 4.6 fusion.24
  581.9 4.0 pad_maximum_fusion
  585.9 12.0 %copy.116 = bf16[4096,1024]{1,0:T(8,128)(2,1)} copy(bf16[4096,1024]{0,1:T(8,128)(2,1)} %pad_maximum_fusion) | data formatting | bytes 16777216
  598.0 4.6 convolution_convert_fusion
  603.5 4.5 convolution_convert_fusion.1
  608.1 257.8 %reduce-scatter.10.cloned.1.call-done = bf16[128,1024]{1,0:T(8,128)(2,1)} async-done(((bf16[4096,1024]{1,0:T(8,128)(2,1)}), bf16[128,1024]{1,0:T(8,128)(2,1)}) %reduce-scatter.10.cloned.1.call-update) | async-done | bytes 262160
  870.1 83.6 %reduce-scatter.8.cloned.1.call-done = bf16[448,512]{1,0:T(8,128)(2,1)} async-done(((bf16[448,4096]{1,0:T(8,128)(2,1)}), bf16[448,512]{1,0:T(8,128)(2,1)}) %reduce-scatter.8.cloned.1.call-update) | async-done | bytes 458768 | tf_op jit(solution)/shard_map/reduce_scatter | solution.py:129
  953.7 52.3 %reduce-scatter.6.cloned.1.call-done = bf16[448,512]{1,0:T(8,128)(2,1)} async-done(((bf16[448,4096]{1,0:T(8,128)(2,1)}), bf16[448,512]{1,0:T(8,128)(2,1)}) %reduce-scatter.6.cloned.1.call-update) | async-done | bytes 458768 | tf_op jit(solution)/shard_map/reduce_scatter | solution.py:78
  (77 shorter events, 35.8 us)
Async XLA Ops:
  7.2 186.7 %copy-start = (bf16[2,128,4096]{2,1,0:T(8,128)(2,1)S(1)}, bf16[2,128,4096]{2,1,0:T(8,128)(2,1)}, u32[]{:S(2)}) copy-start(bf16[2,128,4096]{2,1,0:T(8,128)(2,1)} %param.9) | copy-start | bytes 6291460
  7.2 97.5 %all-gather.5.cloned.1.call-start = ((), (), s32[]{:S(2)}) async-start(), calls=%async_computation.6 | async-start | bytes 2162688 | tf_op jit(solution)/shard_map/all_gather | solution.py:29
  7.9 185.9 %all-gather.7.cloned.1.call-start = ((), (), s32[]{:S(2)}) async-start(), calls=%async_computation.7 | async-start | bytes 2162688 | tf_op jit(solution)/shard_map/all_gather | solution.py:30
  10.3 24.1 %all-to-all-start = ((s32[32,1,1]{2,1,0:T(1,128)}), s32[32,1,1]{2,1,0:T(1,128)S(1)}, u32[]{:S(2)}, u32[]{:S(2)}) async-start(s32[32,1,1]{2,1,0:T(1,128)} %copy.88), calls=%async_computation | async-start | bytes 32768 | tf_op jit(solution)/shard_map/all_to_all | solution.py:47
  24.4 344.1 %all-gather.11.cloned.1.call-start = ((), (), s32[]{:S(2)}) async-start(), calls=%async_computation.9 | async-start | bytes 2162688 | tf_op jit(solution)/shard_map/all_gather | solution.py:31
  204.6 257.7 %all-to-all-start.1 = ((bf16[32,128,512]{2,1,0:T(8,128)(2,1)}), bf16[32,128,512]{2,1,0:T(8,128)(2,1)}, u32[]{:S(2)}, u32[]{:S(2)}) async-start(bf16[32,128,512]{2,1,0:T(8,128)(2,1)} %broadcast_select_fusion), calls=%async_computation.1 | async-start | bytes 8388608 | tf_op jit(solution)/shard_map/all_to_all | solution.py:59
  211.2 247.2 %all-gather.9.cloned.1.call-start = ((), (), s32[]{:S(2)}) async-start(), calls=%async_computation.8 | async-start | bytes 2162688 | tf_op jit(solution)/shard_map/all_gather | solution.py:28
  462.4 8.5 copy-start.5
  487.1 3.5 copy-start.6
  507.6 67.5 %all-to-all-start.2 = ((bf16[32,128,512]{2,1,0:T(8,128)(2,1)}), bf16[32,128,512]{2,1,0:T(8,128)(2,1)}, u32[]{:S(2)}, u32[]{:S(2)}) async-start(bf16[32,128,512]{2,1,0:T(8,128)(2,1)} %copy.106), calls=%async_computation.4 | async-start | bytes 8388608 | tf_op jit(solution)/shard_map/all_to_all | solution.py:115
  514.2 351.7 %reduce-scatter.10.cloned.1.call-start = ((), (), s32[]{:S(2)}) async-start(), calls=%async_computation.12 | async-start | bytes 8650752
  517.4 2.2 copy-start.3
  518.8 3.5 copy-start.7
  519.2 3.0 copy-start.4
  579.7 1.6 copy-start.1
  579.7 2.2 copy-start.2
  598.0 355.7 %reduce-scatter.8.cloned.1.call-start = ((), (), s32[]{:S(2)}) async-start(), calls=%async_computation.11 | async-start | bytes 4128768 | tf_op jit(solution)/shard_map/reduce_scatter | solution.py:129
  602.6 0.9 copy-start.8
  602.6 403.4 %reduce-scatter.6.cloned.1.call-start = ((), (), s32[]{:S(2)}) async-start(), calls=%async_computation.10 | async-start | bytes 4128768 | tf_op jit(solution)/shard_map/reduce_scatter | solution.py:78
Sparse Core Ops, SparseCore 0:
  11.5 93.1 all-gather.4
  108.2 85.6 all-gather.6
  197.1 171.3 all-gather.10
  371.9 86.4 all-gather.8
  598.1 267.7 reduce-scatter.9
  868.9 84.7 reduce-scatter.7
  956.8 49.1 reduce-scatter.5
where the time goes:
time: 1010 us
  waiting for transfers between devices  856 us (85%)
  local copies, waits for them, and re-layouts  57.7 us (6%)
  matrix products  44.6 us (4%)
  starting transfers between devices  27.7 us (3%)
  between operations  14.4 us (1%)
  other arithmetic  12.6 us (1%)
    unnamed x8, waiting for transfers between devices  260 us
    all_gather x1, waiting for transfers between devices, on_device(): lax.all_gather(w_out, 'nbr', axis=1, tiled=True)  157 us
    all_gather x1, waiting for transfers between devices, on_device(): lax.all_gather(w_value, 'nbr', axis=0, tiled=True)  89.2 us
    all_gather x1, waiting for transfers between devices, on_device(): lax.all_gather(w_query, 'nbr', axis=0, tiled=True)  85.9 us
    reduce_scatter x1, waiting for transfers between devices, on_device(): lax.psum_scatter(dx_term.astype(jnp.bfloat16), 'grp', scatter_dimension=1...  83.6 us
    all_gather x1, waiting for transfers between devices, on_device(): lax.all_gather(w_key, 'nbr', axis=0, tiled=True)  68.3 us
    reduce_scatter x1, waiting for transfers between devices, on_device(): lax.psum_scatter(out_term.astype(jnp.bfloat16), 'grp', scatter_dimension=...  52.3 us
    all_to_all x1, waiting for transfers between devices, on_device(): lax.all_to_all(outgoing, 'nbr', split_axis=0, concat_axis=0, tiled=True)  50.2 us
  transfers between devices with their start and end apart: 10, of which 9 were waited for; matrix products, arithmetic and copies ran while one was open for 5% of the time, Pallas kernels for 0%

commit v1 on v0

v1 whole, which is shorter than its diff:
```python
import math

import jax
import jax.numpy as jnp
from jax import lax
from jax.experimental import pallas as pl
from jax.experimental.pallas import tpu as pltpu
from jax.sharding import Mesh, PartitionSpec as P

HS = 128
CH = 64
RLEN = 128
BF = jnp.bfloat16
F32 = jnp.float32
RING = 4
VMEM_LIMIT = 48 * 1024 * 1024


def shift_perm(axis, k):
    n = lax.axis_size(axis)
    return [(i, (i + k) % n) for i in range(n)]


def fetch(value, axis, k):
    return lax.ppermute(value, axis, shift_perm(axis, -k))


def deliver(value, axis, k):
    return lax.ppermute(value, axis, shift_perm(axis, k))


def swap(value, axis, bit=1):
    n = lax.axis_size(axis)
    return lax.ppermute(value, axis, [(i, i ^ bit) for i in range(n)])


def ring_gather_direct(value, axis):
    return [value] + [fetch(value, axis, k) for k in range(1, RING)]


def ring_gather_forward(value, axis):
    half = value.shape[0] // 2
    ahead = fetch(value, axis, 1)
    behind = fetch(value, axis, -1)
    far_a = fetch(ahead[:half], axis, 1)
    far_b = fetch(behind[half:], axis, -1)
    return [value, ahead, far_a, far_b, behind]


def ring_sum(parts, axis):
    total = parts[0].astype(F32)
    for k in range(1, RING):
        total = total + deliver(parts[k], axis, k).astype(F32)
    return total


def reorder_kernel(places, src, dst):
    for j in range(src.shape[1] // 128):
        start = pl.multiple_of(places[j] * 128, 128)
        dst[:, j * 128 : (j + 1) * 128] = src[:, pl.ds(start, 128)]


def reorder(rows, places):
    return pl.pallas_call(
        reorder_kernel,
        out_shape=jax.ShapeDtypeStruct(rows.shape, rows.dtype),
        in_specs=[
            pl.BlockSpec(memory_space=pltpu.SMEM),
            pl.BlockSpec(memory_space=pltpu.VMEM),
        ],
        out_specs=pl.BlockSpec(memory_space=pltpu.VMEM),
        compiler_params=pltpu.CompilerParams(vmem_limit_bytes=VMEM_LIMIT),
        name="reorder",
    )(places, rows)


def dot_nt(a, b):
    return lax.dot_general(a, b, (((1,), (1,)), ((), ())), preferred_element_type=F32)


def dot_tn(a, b):
    return lax.dot_general(a, b, (((0,), (0,)), ((), ())), preferred_element_type=F32)


def dot_nn(a, b):
    return jnp.dot(a, b, preferred_element_type=F32)


def attention_kernel(
    pos_p, pos_q, query, d_ctx, kv_p, kv_q, context, d_query, d_kv_p, d_kv_q, ctx_f, dq_f
):
    scale = 1.0 / math.sqrt(HS)
    spans = query.shape[0] // CH
    for head, (pos, kv, d_kv) in enumerate(((pos_p, kv_p, d_kv_p), (pos_q, kv_q, d_kv_q))):
        cols = slice(head * HS, (head + 1) * HS)
        for c in range(spans):
            rows = slice(c * CH, (c + 1) * CH)
            first, second = pos[2 * c], pos[2 * c + 1]
            q = query[rows, cols]
            dc = d_ctx[rows, cols]
            keys = jnp.concatenate([kv[first, :, :HS], kv[second, :, :HS]], 0)
            values = jnp.concatenate([kv[first, :, HS:], kv[second, :, HS:]], 0)
            raised = jnp.exp(dot_nt(q, keys) * scale)
            probs = raised / jnp.sum(raised, -1, keepdims=True)
            low = probs.astype(BF)
            ctx_f[rows, cols] = dot_nn(low, values)
            d_probs = dot_nt(dc, values)
            row_dot = jnp.sum(probs * d_probs, -1, keepdims=True)
            d_scores = (probs * (d_probs - row_dot)).astype(BF)
            dq_f[rows, cols] = dot_nn(d_scores, keys) * scale
            d_keys = (dot_tn(d_scores, q) * scale).astype(BF)
            d_values = dot_tn(low, dc).astype(BF)
            d_kv[first, :, :HS] = d_keys[:RLEN]
            d_kv[first, :, HS:] = d_values[:RLEN]
            d_kv[second, :, :HS] = d_keys[RLEN:]
            d_kv[second, :, HS:] = d_values[RLEN:]
    row = lax.broadcasted_iota(jnp.int32, ctx_f.shape, 0)
    for src, dst in ((ctx_f, context), (dq_f, d_query)):
        moved = pltpu.roll(src[...], CH - 1, 0)
        dst[...] = jnp.where(row >= CH - 1, moved, 0.0).astype(BF)


def attention(pos_p, pos_q, query, d_ctx, kv_p, kv_q):
    rows = jax.ShapeDtypeStruct(query.shape, BF)
    smem = pl.BlockSpec(memory_space=pltpu.SMEM)
    vmem = pl.BlockSpec(memory_space=pltpu.VMEM)
    return pl.pallas_call(
        attention_kernel,
        out_shape=(
            rows,
            rows,
            jax.ShapeDtypeStruct(kv_p.shape, BF),
            jax.ShapeDtypeStruct(kv_q.shape, BF),
        ),
        in_specs=[smem, smem, vmem, vmem, vmem, vmem],
        out_specs=(vmem, vmem, vmem, vmem),
        scratch_shapes=[pltpu.VMEM(query.shape, F32), pltpu.VMEM(query.shape, F32)],
        compiler_params=pltpu.CompilerParams(vmem_limit_bytes=VMEM_LIMIT),
        name="attention",
    )(pos_p, pos_q, query, d_ctx, kv_p, kv_q)


def shift_in(rows):
    filler = jnp.zeros((CH - 1,) + rows.shape[1:], rows.dtype)
    return jnp.concatenate([rows[CH - 1 :], filler], 0)


def pick(flags, ones, zeros):
    return jnp.where(flags[..., None, None] == 1, ones, zeros)


def on_device(tokens, encoded, neighbour_ids, w_query, w_key, w_value, w_out, d_out):
    me_x, me_y, me_zh = lax.axis_index("x"), lax.axis_index("y"), lax.axis_index("zh")
    me_zl, me_c = lax.axis_index("zl"), lax.axis_index("c")
    k4 = jnp.arange(RING, dtype=jnp.int32)
    k2 = jnp.arange(2, dtype=jnp.int32)
    cols = w_query.shape[1]
    width = tokens.shape[2]
    chunk = width // 32

    def block_number(zh, y, x):
        return zh * 16 + y * 4 + x

    places_a = block_number(
        (me_zh ^ k2)[None, None, :],
        ((me_y + k4) % RING)[None, :, None],
        ((me_x + k4) % RING)[:, None, None],
    ).reshape(32)
    places_b = block_number(
        (me_zh ^ k2)[None, None, :],
        ((me_y + k4) % RING)[:, None, None],
        ((me_x + k4) % RING)[None, :, None],
    ).reshape(32)

    def position(zh, y, x):
        kx, ky, zr = (x - me_x) % RING, (y - me_y) % RING, zh ^ me_zh
        return kx * 8 + ky * 2 + zr, ky * 8 + kx * 2 + zr

    wanted = neighbour_ids[0].reshape(-1)
    block = wanted // 2
    pos_a, pos_b = position(block // 16, (block // 4) % 4, block % 4)
    hit = block[None, :] == jnp.arange(32, dtype=jnp.int32)[:, None]
    asking = jnp.sum(jnp.where(hit, (wanted % 2)[None, :] + 1, 0), axis=1).astype(jnp.int32)
    asked_y = jnp.stack(ring_gather_direct(asking, "y"))
    asked_x = jnp.stack(ring_gather_direct(asking, "x"))

    def local_order(asked, zr):
        flipped = jnp.where(asked > 0, ((asked - 1) ^ me_c) + 1, 0)
        return jnp.where(zr == 1, flipped, asked)

    row_blocks = block_number((me_zh ^ k2)[None, :], me_y, ((me_x + k4) % RING)[:, None])
    col_blocks = block_number((me_zh ^ k2)[None, :], ((me_y + k4) % RING)[:, None], me_x)
    asked_p = local_order(asked_y[:, row_blocks], k2[None, None, :])
    asked_q = local_order(asked_x[:, col_blocks], k2[None, None, :])

    group_a = jnp.concatenate([w_query, w_key], 1)
    group_b = jnp.concatenate([w_out.T, w_value], 1)
    both = jnp.stack([group_a, group_b])
    other = swap(both, "zh")
    shard_a = jnp.stack([both[0], other[0]])
    shard_b = jnp.stack([both[1], other[1]])
    stage_a = jnp.stack(ring_gather_direct(shard_a, "y"))
    stage_b = jnp.stack(ring_gather_direct(shard_b, "x"))
    full_a = jnp.concatenate(ring_gather_forward(stage_a, "x"), 0)
    full_b = jnp.concatenate(ring_gather_forward(stage_b, "y"), 0)
    full_a = full_a.reshape(width, 2 * cols)
    full_b = full_b.reshape(width, 2 * cols)
    wq, wk = full_a[:, :cols], full_a[:, cols:]
    wo, wv = full_b[:, :cols], full_b[:, cols:]

    far = swap(encoded[me_c], "zh")
    far_pair = swap(far, "c")
    enc_all = jnp.concatenate([encoded[0], encoded[1], far, far_pair], 0)
    enc_a = reorder(enc_all, places_a)
    enc_b = reorder(enc_all, places_b)
    tok_a = reorder(tokens[0], places_a)
    up_b = reorder(d_out[0], places_b)

    keys = dot_nn(enc_a, wk).astype(BF).reshape(2, 2, RLEN, cols)
    values = dot_nn(enc_b, wv).astype(BF).reshape(2, 2, RLEN, cols)
    table_p = jnp.concatenate([keys[..., :HS], values[..., :HS]], -1)
    table_q = jnp.concatenate([keys[..., HS:], values[..., HS:]], -1)
    row_p = jnp.stack(ring_gather_direct(table_p, "x"))
    row_q = jnp.stack(ring_gather_direct(table_q, "y"))
    send_p = [pick(asked_p[k] - 1, row_p[:, :, 1], row_p[:, :, 0]) for k in range(RING)]
    send_q = [pick(asked_q[k] - 1, row_q[:, :, 1], row_q[:, :, 0]) for k in range(RING)]
    kv_p = jnp.stack([send_p[0]] + [fetch(send_p[RING - k], "y", k) for k in range(1, RING)])
    kv_q = jnp.stack([send_q[0]] + [fetch(send_q[RING - k], "x", k) for k in range(1, RING)])
    kv_p = kv_p.reshape(32, RLEN, 2 * HS)
    kv_q = kv_q.reshape(32, RLEN, 2 * HS)

    query = shift_in(dot_nn(tok_a, wq).astype(BF))
    d_context = shift_in(dot_nn(up_b, wo).astype(BF))

    context, d_query, d_kv_p, d_kv_q = attention(pos_b, pos_a, query, d_context, kv_p, kv_q)

    def return_grads(d_kv, asked, first, second):
        parts = d_kv.reshape(RING, RING, 2, RLEN, 2 * HS)
        total = [0.0, 0.0]
        for k in range(RING):
            came = parts[0] if k == 0 else deliver(parts[k], first, k)
            flags = asked[(RING - k) % RING]
            for e in range(2):
                total[e] = total[e] + pick(
                    (flags == e + 1).astype(jnp.int32), came.astype(F32), jnp.zeros((), F32)
                )
        low = jnp.stack(total, 2).astype(BF)
        return ring_sum([low[k] for k in range(RING)], second).astype(BF)

    grads_p = return_grads(d_kv_p, asked_p, "y", "x")
    grads_q = return_grads(d_kv_q, asked_q, "x", "y")

    lr, hr = k2[None, :, None, None], k2[None, None, :, None]
    part_c = me_c ^ k2[:, None, None, None]
    part_lo, part_hi = (me_zl % 2) ^ lr, (me_zl // 2) ^ hr
    chosen_a, chosen_b = position(part_hi, 2 * part_lo + part_c, k4[None, None, None, :])
    wq_cols = wq.reshape(32, chunk, cols)[chosen_a.reshape(32)].reshape(8, 4 * chunk, cols)
    wo_cols = wo.reshape(32, chunk, cols)[chosen_b.reshape(32)].reshape(8, 4 * chunk, cols)

    def group_sum(rows, weights):
        term = jnp.einsum("te,pde->ptd", rows, weights, preferred_element_type=F32).astype(BF)
        half = (term[:4].astype(F32) + swap(term[4:], "c").astype(F32)).astype(BF)
        pair = (half[:2].astype(F32) + swap(half[2:], "zl", 1).astype(F32)).astype(BF)
        return (pair[0].astype(F32) + swap(pair[1], "zl", 2).astype(F32)).astype(BF)

    attended = group_sum(context, wo_cols)
    d_tokens = group_sum(d_query, wq_cols)

    def block_sum(term, first, second):
        parts = term.reshape(RING, RING, 2, chunk, cols)
        line = ring_sum([parts[k] for k in range(RING)], first).astype(BF)
        return ring_sum([line[k] for k in range(RING)], second).astype(BF)

    def halves_sum(a, b):
        mine = jnp.stack([a[0], b[0]]).astype(F32)
        return mine + swap(jnp.stack([a[1], b[1]]), "zh").astype(F32)

    sum_query = block_sum(dot_tn(tok_a, d_query).astype(BF), "x", "y")
    sum_out = block_sum(dot_tn(up_b, context).astype(BF), "y", "x")
    grad_query, grad_out = halves_sum(sum_query, sum_out)

    rows = 4 * RLEN
    grads_k = jnp.concatenate([grads_p[..., :HS], grads_q[..., :HS]], -1).reshape(rows, cols)
    grads_v = jnp.concatenate([grads_p[..., HS:], grads_q[..., HS:]], -1).reshape(rows, cols)
    sum_key = block_sum(dot_tn(enc_a, grads_k).astype(BF), "x", "y")
    sum_value = block_sum(dot_tn(enc_b, grads_v).astype(BF), "y", "x")
    grad_key, grad_value = halves_sum(sum_key, sum_value)

    return attended[None], d_tokens[None], grad_query, grad_key, grad_value, grad_out.T


def solution(mesh):
    grid = Mesh(mesh.devices.reshape(4, 2, 2, 4, 4), ("zl", "c", "zh", "y", "x"))
    grp, nbr = ("zl", "c"), ("zh", "y", "x")
    in_specs = (
        P(nbr, None, None),
        P(nbr, None, None),
        P(nbr, None, None),
        P(nbr, grp),
        P(nbr, grp),
        P(nbr, grp),
        P(grp, nbr),
        P(nbr, None, None),
    )
    out_specs = (
        P(nbr, None, grp),
        P(nbr, None, grp),
        P(nbr, grp),
        P(nbr, grp),
        P(nbr, grp),
        P(grp, nbr),
    )
    return jax.shard_map(
        on_device, mesh=grid, in_specs=in_specs, out_specs=out_specs, check_vma=False
    )
```

time: 1010 us -> 459 us (0.45); the launches traced: 1010 us -> 450 us
  waiting for transfers between devices: 856 us -> 156 us
  starting transfers between devices: 27.7 us -> 191 us
  matrix products: 44.6 us -> 15.6 us
  Pallas kernels: 0 us -> 21 us
  local copies, waits for them, and re-layouts: 57.7 us -> 39.5 us
  other arithmetic: 12.6 us -> 24.9 us
  between operations: 14.4 us -> 2.12 us
    all_gather x4 -> x0, waiting for transfers between devices: 400 us -> none  [the longest x1 157 us: on_device(): lax.all_gather(w_out, 'nbr', axis=1, tiled=True)]
    unnamed x8 -> x0, waiting for transfers between devices: 260 us -> none
    ppermute x0 -> x79, starting transfers between devices: none -> 191 us  [the longest x36 73.1 us: deliver(): return lax.ppermute(value, axis, shift_perm(axis, k))]
    ppermute x0 -> x79, waiting for transfers between devices: none -> 156 us  [the longest x36 78 us: deliver(): return lax.ppermute(value, axis, shift_perm(axis, k))]
    reduce_scatter x2 -> x0, waiting for transfers between devices: 136 us -> none  [the longest x1 83.6 us: on_device(): lax.psum_scatter(dx_term.astype(jnp.bfloat16), 'grp', scatter_dimension=1...]
    all_to_all x3 -> x0, waiting for transfers between devices: 59.5 us -> none  [the longest x1 50.2 us: on_device(): lax.all_to_all(outgoing, 'nbr', split_axis=0, concat_axis=0, tiled=True)]
    dot_general x16 -> x10, matrix products: 44.6 us -> 15.6 us  [the longest x4 7.97 us: dot_nn(): return jnp.dot(a, b, preferred_element_type=F32)]
    all_to_all x3 -> x0, starting transfers between devices: 27.2 us -> none  [the longest x1 14 us: on_device(): lax.all_to_all(asking[:, None], 'nbr', split_axis=0, concat_axis=0, tiled...]
  transfers between devices with their start and end apart: 10 -> 79, of which waited for: 9 -> 32; matrix products, arithmetic and copies ran while one was open for 5% -> 14% of each run, Pallas kernels for 0% -> 3%
where the time goes in v1:
time: 459 us; the launch traced here: 450 us
  starting transfers between devices  191 us (42%)
  waiting for transfers between devices  156 us (34%)
  local copies, waits for them, and re-layouts  39.5 us (9%)
  other arithmetic  24.9 us (5%)
  Pallas kernels  21 us (5%)
  matrix products  15.6 us (3%)
    ppermute x36, waiting for transfers between devices, deliver(): return lax.ppermute(value, axis, shift_perm(axis, k))  78 us
    ppermute x36, starting transfers between devices, deliver(): return lax.ppermute(value, axis, shift_perm(axis, k))  73.1 us
    ppermute x11, starting transfers between devices, swap(): return lax.ppermute(value, axis, [(i, i ^ bit) for i in range(n)])  64.5 us
    ppermute x32, starting transfers between devices, fetch(): return lax.ppermute(value, axis, shift_perm(axis, -k))  53.4 us
    ppermute x11, waiting for transfers between devices, swap(): return lax.ppermute(value, axis, [(i, i ^ bit) for i in range(n)])  52.3 us
    ppermute x32, waiting for transfers between devices, fetch(): return lax.ppermute(value, axis, shift_perm(axis, -k))  25.7 us
    unnamed x43, local copies, waits for them, and re-layouts  16.4 us
    pallas_call x4, Pallas kernels, reorder(): pl.pallas_call(reorder_kernel, out_shape=jax.ShapeDtypeStruct(rows.shape,...  12.8 us
  transfers between devices with their start and end apart: 79, of which 32 were waited for; matrix products, arithmetic and copies ran while one was open for 14% of the time, Pallas kernels for 3%

profile of v1, /device:TPU:16, one launch (start us, length us, event | category | flops | bytes accessed | tf_op | source)
XLA Modules:
  0.0 450.1 jit_solution(14941561438197445417)
XLA Ops:
  26.1 7.2 %collective-permute-start = (bf16[2,128,512]{2,1,0:T(8,128)(2,1)}, bf16[2,128,512]{2,1,0:T(8,128)(2,1)}, u32[]{:S(2)}, u32[]{:S(2)}) collective-permute-start(bf16[2,128,512]{2,1,0:T(8,128)(2,1)} %pad_maximum_fusion.8), channel_id=1, source_target_pairs={{0,16},{16,0},{1,17},{17,1},{2,18},{18,2},{3,19},{19,3},{4,20},{20... | collective-permute-start | bytes 786440 | tf_op jit(solution)/shard_map/ppermute | solution.py:34
  34.7 4.7 %collective-permute-done = bf16[2,128,512]{2,1,0:T(8,128)(2,1)} collective-permute-done((bf16[2,128,512]{2,1,0:T(8,128)(2,1)}, bf16[2,128,512]{2,1,0:T(8,128)(2,1)}, u32[]{:S(2)}, u32[]{:S(2)}) %collective-permute-start) | collective-permute-done | bytes 262176 | tf_op jit(solution)/shard_map/ppermute | solution.py:34
  52.7 9.2 %collective-permute-start.18 = (bf16[128,4096]{1,0:T(8,128)(2,1)S(1)}, bf16[128,4096]{1,0:T(8,128)(2,1)S(1)}, u32[]{:S(2)}, u32[]{:S(2)}) collective-permute-start(bf16[128,4096]{1,0:T(8,128)(2,1)S(1)} %get-tuple-element.90), channel_id=1, source_target_pairs={{0,16},{16,0},{1,17},{17,1},{2,18},{18,2},{3,19},{19,3},{4,20},{20... | collective-permute-start | bytes 3145736 | tf_op jit(solution)/shard_map/ppermute | solution.py:34
  70.4 6.1 %collective-permute-done.18 = bf16[128,4096]{1,0:T(8,128)(2,1)S(1)} collective-permute-done((bf16[128,4096]{1,0:T(8,128)(2,1)S(1)}, bf16[128,4096]{1,0:T(8,128)(2,1)S(1)}, u32[]{:S(2)}, u32[]{:S(2)}) %collective-permute-start.18) | collective-permute-done | bytes 1048608 | tf_op jit(solution)/shard_map/ppermute | solution.py:34
  76.5 4.1 collective-permute-done.4
  82.2 3.6 collective-permute-start.7
  111.0 5.7 %collective-permute-start.30 = (bf16[2,2,128,256]{3,2,0,1:T(8,128)(2,1)S(1)}, bf16[2,2,128,256]{3,2,0,1:T(8,128)(2,1)S(1)}, u32[]{:S(2)}, u32[]{:S(2)}) collective-permute-start(bf16[2,2,128,256]{3,2,0,1:T(8,128)(2,1)S(1)} %get-tuple-element.125), channel_id=1, source_target_pairs={{0,8},{4,12},{8,0},{12,4},{1,9},{5,13},{9,1},{13,5},{2,10},{6,14},... | collective-permute-start | bytes 786440 | tf_op jit(solution)/shard_map/ppermute | solution.py:25
  126.3 3.5 collective-permute-start.32
  135.6 3.6 gather_fusion
  139.2 3.7 gather_fusion.3
  151.2 4.3 collective-permute-done.34
  155.5 12.9 %collective-permute-done.33 = bf16[4,2,128,256]{3,2,1,0:T(8,128)(2,1)S(1)} collective-permute-done((bf16[4,2,128,256]{3,2,1,0:T(8,128)(2,1)S(1)}, bf16[4,2,128,256]{3,2,1,0:T(8,128)(2,1)S(1)}, u32[]{:S(2)}, u32[]{:S(2)}) %collective-permute-start.33) | collective-permute-done | bytes 524320 | tf_op jit(solution)/shard_map/ppermute | solution.py:25
  175.1 8.2 %attention.1 = (bf16[448,256]{1,0:T(8,128)(2,1)S(1)}, bf16[448,256]{1,0:T(8,128)(2,1)S(1)}, bf16[32,128,256]{2,1,0:T(8,128)(2,1)S(1)}, bf16[32,128,256]{2,1,0:T(8,128)(2,1)S(1)}) custom-call(s32[14]{0:T(128)S(1)} %add_add_fusion.1.pos_p, s32[14]{0:T(128)S(1)} %get-tuple-element.56.pos_q, bf16[448,256]{1,0:T(8,128)(2,1)S(1)} %concatenate.39.query, ...), custom_call_target="tpu_custom_call" | custom-call | tf_op jit(solution)/shard_map/attention/pallas_call | solution.py:127
  198.0 6.8 %collective-permute-done.56 = bf16[4,2,128,256]{3,2,1,0:T(8,128)(2,1)S(1)} collective-permute-done((bf16[4,2,128,256]{3,2,1,0:T(8,128)(2,1)S(1)}, bf16[4,2,128,256]{3,2,1,0:T(8,128)(2,1)S(1)}, u32[]{:S(2)}, u32[]{:S(2)}) %collective-permute-start.56) | collective-permute-done | bytes 524320 | tf_op jit(solution)/shard_map/ppermute | solution.py:29
  206.8 8.8 %collective-permute-start.49 = (bf16[4,2,128,256]{3,2,1,0:T(8,128)(2,1)S(1)}, bf16[4,2,128,256]{3,2,1,0:T(8,128)(2,1)S(1)}, u32[]{:S(2)}, u32[]{:S(2)}) collective-permute-start(bf16[4,2,128,256]{3,2,1,0:T(8,128)(2,1)S(1)} %bitcast.312), channel_id=1, source_target_pairs={{0,12},{4,0},{8,4},{12,8},{1,13},{5,1},{9,5},{13,9},{2,14},{6,2},{... | collective-permute-start | bytes 1572872 | tf_op jit(solution)/shard_map/ppermute | solution.py:29
  220.2 14.7 %collective-permute-done.49 = bf16[4,2,128,256]{3,2,1,0:T(8,128)(2,1)S(1)} collective-permute-done((bf16[4,2,128,256]{3,2,1,0:T(8,128)(2,1)S(1)}, bf16[4,2,128,256]{3,2,1,0:T(8,128)(2,1)S(1)}, u32[]{:S(2)}, u32[]{:S(2)}) %collective-permute-start.49) | collective-permute-done | bytes 524320 | tf_op jit(solution)/shard_map/ppermute | solution.py:29
  240.2 10.0 %collective-permute-done.62 = bf16[4,2,128,256]{3,2,1,0:T(8,128)(2,1)S(1)} collective-permute-done((bf16[4,2,128,256]{3,2,1,0:T(8,128)(2,1)S(1)}, bf16[4,2,128,256]{3,2,1,0:T(8,128)(2,1)S(1)}, u32[]{:S(2)}, u32[]{:S(2)}) %collective-permute-start.62) | collective-permute-done | bytes 524320 | tf_op jit(solution)/shard_map/ppermute | solution.py:29
  250.2 5.7 %collective-permute-start.44 = (bf16[2,128,256]{2,1,0:T(8,128)(2,1)S(1)}, bf16[2,128,256]{2,1,0:T(8,128)(2,1)S(1)}, u32[]{:S(2)}, u32[]{:S(2)}) collective-permute-start(bf16[2,128,256]{2,1,0:T(8,128)(2,1)S(1)} %get-tuple-element.110), channel_id=1, source_target_pairs={{0,4},{4,8},{8,12},{12,0},{1,5},{5,9},{9,13},{13,1},{2,6},{6,10},{... | collective-permute-start | bytes 393224 | tf_op jit(solution)/shard_map/ppermute | solution.py:29
  265.2 3.6 collective-permute-done.50
  268.8 6.6 %collective-permute-start.59 = (bf16[2,2,128,256]{3,2,1,0:T(8,128)(2,1)S(1)}, bf16[2,2,128,256]{3,2,1,0:T(8,128)(2,1)S(1)}, u32[]{:S(2)}, u32[]{:S(2)}) collective-permute-start(bf16[2,2,128,256]{3,2,1,0:T(8,128)(2,1)S(1)} %get-tuple-element.93), channel_id=1, source_target_pairs={{0,3},{1,0},{2,1},{3,2},{4,7},{5,4},{6,5},{7,6},{8,11},{9,8},{10,9... | collective-permute-start | bytes 786440 | tf_op jit(solution)/shard_map/ppermute | solution.py:29
  277.7 4.4 collective-permute-done.59
  299.9 8.2 %collective-permute-done.74 = bf16[4,2,128,256]{3,2,1,0:T(8,128)(2,1)S(1)} collective-permute-done((bf16[4,2,128,256]{3,2,1,0:T(8,128)(2,1)S(1)}, bf16[4,2,128,256]{3,2,1,0:T(8,128)(2,1)S(1)}, u32[]{:S(2)}, u32[]{:S(2)}) %collective-permute-start.74) | collective-permute-done | bytes 524320 | tf_op jit(solution)/shard_map/ppermute | solution.py:29
  308.1 9.0 %collective-permute-start.68 = (bf16[4,2,128,256]{3,2,1,0:T(8,128)(2,1)S(1)}, bf16[4,2,128,256]{3,2,1,0:T(8,128)(2,1)S(1)}, u32[]{:S(2)}, u32[]{:S(2)}) collective-permute-start(bf16[4,2,128,256]{3,2,1,0:T(8,128)(2,1)S(1)} %bitcast.325), channel_id=1, source_target_pairs={{0,3},{1,0},{2,1},{3,2},{4,7},{5,4},{6,5},{7,6},{8,11},{9,8},{10,9... | collective-permute-start | bytes 1572872 | tf_op jit(solution)/shard_map/ppermute | solution.py:29
  320.8 12.6 %collective-permute-done.68 = bf16[4,2,128,256]{3,2,1,0:T(8,128)(2,1)S(1)} collective-permute-done((bf16[4,2,128,256]{3,2,1,0:T(8,128)(2,1)S(1)}, bf16[4,2,128,256]{3,2,1,0:T(8,128)(2,1)S(1)}, u32[]{:S(2)}, u32[]{:S(2)}) %collective-permute-start.68) | collective-permute-done | bytes 524320 | tf_op jit(solution)/shard_map/ppermute | solution.py:29
  333.4 3.7 collective-permute-start.77
  351.0 25.7 %collective-permute-start.36 = (bf16[2,448,512]{2,1,0:T(8,128)(2,1)S(1)}, bf16[2,448,512]{2,1,0:T(8,128)(2,1)}, u32[]{:S(2)}, u32[]{:S(2)}) collective-permute-start(bf16[2,448,512]{2,1,0:T(8,128)(2,1)S(1)} %slice.491), channel_id=1, source_target_pairs={{0,64},{64,0},{128,192},{192,128},{1,65},{65,1},{129,193},{193,129... | collective-permute-start | bytes 2752520 | tf_op jit(solution)/shard_map/ppermute | solution.py:34
  384.4 21.2 %collective-permute-done.78 = bf16[2,128,256]{2,1,0:T(8,128)(2,1)S(1)} collective-permute-done((bf16[2,128,256]{2,1,0:T(8,128)(2,1)S(1)}, bf16[2,128,256]{2,1,0:T(8,128)(2,1)S(1)}, u32[]{:S(2)}, u32[]{:S(2)}) %collective-permute-start.78) | collective-permute-done | bytes 131104 | tf_op jit(solution)/shard_map/ppermute | solution.py:34
  407.1 8.1 %collective-permute-start.37 = (bf16[448,512]{1,0:T(8,128)(2,1)S(1)}, bf16[448,512]{1,0:T(8,128)(2,1)S(1)}, u32[]{:S(2)}, u32[]{:S(2)}) collective-permute-start(bf16[448,512]{1,0:T(8,128)(2,1)S(1)} %slice_bitcast_fusion.4), channel_id=1, source_target_pairs={{0,128},{64,192},{128,0},{192,64},{1,129},{65,193},{129,1},{193,65... | collective-permute-start | bytes 1376264 | tf_op jit(solution)/shard_map/ppermute | solution.py:34
  415.2 3.6 collective-permute-done.39
  420.2 10.2 %collective-permute-start.40 = (bf16[448,512]{1,0:T(8,128)(2,1)S(1)}, bf16[448,512]{1,0:T(8,128)(2,1)S(1)}, u32[]{:S(2)}, u32[]{:S(2)}) collective-permute-start(bf16[448,512]{1,0:T(8,128)(2,1)S(1)} %slice_bitcast_fusion.2), channel_id=1, source_target_pairs={{0,128},{64,192},{128,0},{192,64},{1,129},{65,193},{129,1},{193,65... | collective-permute-start | bytes 1376264 | tf_op jit(solution)/shard_map/ppermute | solution.py:34
  431.2 11.5 %collective-permute-done.37 = bf16[448,512]{1,0:T(8,128)(2,1)S(1)} collective-permute-done((bf16[448,512]{1,0:T(8,128)(2,1)S(1)}, bf16[448,512]{1,0:T(8,128)(2,1)S(1)}, u32[]{:S(2)}, u32[]{:S(2)}) %collective-permute-start.37) | collective-permute-done | bytes 458784 | tf_op jit(solution)/shard_map/ppermute | solution.py:34
  443.6 5.2 %collective-permute-done.40 = bf16[448,512]{1,0:T(8,128)(2,1)S(1)} collective-permute-done((bf16[448,512]{1,0:T(8,128)(2,1)S(1)}, bf16[448,512]{1,0:T(8,128)(2,1)S(1)}, u32[]{:S(2)}, u32[]{:S(2)}) %collective-permute-start.40) | collective-permute-done | bytes 458784 | tf_op jit(solution)/shard_map/ppermute | solution.py:34
  (309 shorter events, 191.6 us)
Async XLA Ops:
  1.6 23.4 %collective-permute-start.28 = (s32[32]{0:T(128)S(1)}, s32[32]{0:T(128)S(1)}, u32[]{:S(2)}, u32[]{:S(2)}) collective-permute-start(s32[32]{0:T(128)S(1)} %select_reduce_fusion), channel_id=1, source_target_pairs={{0,1},{1,2},{2,3},{3,0},{4,5},{5,6},{6,7},{7,4},{8,9},{9,10},{10,1... | collective-permute-start | bytes 392 | tf_op jit(solution)/shard_map/ppermute | solution.py:25
  3.2 22.9 %collective-permute-start.27 = (s32[32]{0:T(128)S(1)}, s32[32]{0:T(128)S(1)}, u32[]{:S(2)}, u32[]{:S(2)}) collective-permute-start(s32[32]{0:T(128)S(1)} %select_reduce_fusion), channel_id=1, source_target_pairs={{0,2},{1,3},{2,0},{3,1},{4,6},{5,7},{6,4},{7,5},{8,10},{9,11},{10,... | collective-permute-start | bytes 392 | tf_op jit(solution)/shard_map/ppermute | solution.py:25
  5.9 27.4 %collective-permute-start.26 = (s32[32]{0:T(128)S(1)}, s32[32]{0:T(128)S(1)}, u32[]{:S(2)}, u32[]{:S(2)}) collective-permute-start(s32[32]{0:T(128)S(1)} %select_reduce_fusion), channel_id=1, source_target_pairs={{0,3},{1,0},{2,1},{3,2},{4,7},{5,4},{6,5},{7,6},{8,11},{9,8},{10,9... | collective-permute-start | bytes 392 | tf_op jit(solution)/shard_map/ppermute | solution.py:25
  7.3 25.9 %collective-permute-start.17 = (s32[32]{0:T(128)S(1)}, s32[32]{0:T(128)S(1)}, u32[]{:S(2)}, u32[]{:S(2)}) collective-permute-start(s32[32]{0:T(128)S(1)} %select_reduce_fusion), channel_id=1, source_target_pairs={{0,4},{4,8},{8,12},{12,0},{1,5},{5,9},{9,13},{13,1},{2,6},{6,10},{... | collective-permute-start | bytes 392 | tf_op jit(solution)/shard_map/ppermute | solution.py:25
  8.6 24.7 %collective-permute-start.16 = (s32[32]{0:T(128)S(1)}, s32[32]{0:T(128)S(1)}, u32[]{:S(2)}, u32[]{:S(2)}) collective-permute-start(s32[32]{0:T(128)S(1)} %select_reduce_fusion), channel_id=1, source_target_pairs={{0,8},{4,12},{8,0},{12,4},{1,9},{5,13},{9,1},{13,5},{2,10},{6,14},... | collective-permute-start | bytes 392 | tf_op jit(solution)/shard_map/ppermute | solution.py:25
  52.7 23.8 %collective-permute-start.18 = (bf16[128,4096]{1,0:T(8,128)(2,1)S(1)}, bf16[128,4096]{1,0:T(8,128)(2,1)S(1)}, u32[]{:S(2)}, u32[]{:S(2)}) collective-permute-start(bf16[128,4096]{1,0:T(8,128)(2,1)S(1)} %get-tuple-element.90), channel_id=1, source_target_pairs={{0,16},{16,0},{1,17},{17,1},{2,18},{18,2},{3,19},{19,3},{4,20},{20... | collective-permute-start | bytes 3145736 | tf_op jit(solution)/shard_map/ppermute | solution.py:34
  62.4 23.5 %collective-permute-start.13 = (bf16[4,2,128,512]{3,2,1,0:T(8,128)(2,1)S(1)}, bf16[4,2,128,512]{3,2,1,0:T(8,128)(2,1)S(1)}, u32[]{:S(2)}, u32[]{:S(2)}) collective-permute-start(bf16[4,2,128,512]{3,2,1,0:T(8,128)(2,1)S(1)} %pad_maximum_fusion.4), channel_id=1, source_target_pairs={{0,1},{1,2},{2,3},{3,0},{4,5},{5,6},{6,7},{7,4},{8,9},{9,10},{10,1... | collective-permute-start | bytes 3145736 | tf_op jit(solution)/shard_map/ppermute | solution.py:25
  64.1 21.9 %collective-permute-start.11 = (bf16[4,2,128,512]{3,2,1,0:T(8,128)(2,1)S(1)}, bf16[4,2,128,512]{3,2,1,0:T(8,128)(2,1)S(1)}, u32[]{:S(2)}, u32[]{:S(2)}) collective-permute-start(bf16[4,2,128,512]{3,2,1,0:T(8,128)(2,1)S(1)} %pad_maximum_fusion.4), channel_id=1, source_target_pairs={{0,3},{1,0},{2,1},{3,2},{4,7},{5,4},{6,5},{7,6},{8,11},{9,8},{10,9... | collective-permute-start | bytes 3145736 | tf_op jit(solution)/shard_map/ppermute | solution.py:25
  85.9 23.1 %collective-permute-start.14 = (bf16[2,2,128,512]{3,2,1,0:T(8,128)(2,1)S(1)}, bf16[2,2,128,512]{3,2,1,0:T(8,128)(2,1)S(1)}, u32[]{:S(2)}, u32[]{:S(2)}) collective-permute-start(bf16[2,2,128,512]{3,2,1,0:T(8,128)(2,1)S(1)} %slice.466), channel_id=1, source_target_pairs={{0,1},{1,2},{2,3},{3,0},{4,5},{5,6},{6,7},{7,4},{8,9},{9,10},{10,1... | collective-permute-start | bytes 1572872 | tf_op jit(solution)/shard_map/ppermute | solution.py:25
  86.8 22.1 %collective-permute-start.12 = (bf16[2,2,128,512]{3,2,1,0:T(8,128)(2,1)}, bf16[2,2,128,512]{3,2,1,0:T(8,128)(2,1)S(1)}, u32[]{:S(2)}, u32[]{:S(2)}) collective-permute-start(bf16[2,2,128,512]{3,2,1,0:T(8,128)(2,1)} %slice.465), channel_id=1, source_target_pairs={{0,3},{1,0},{2,1},{3,2},{4,7},{5,4},{6,5},{7,6},{8,11},{9,8},{10,9... | collective-permute-start | bytes 1572872 | tf_op jit(solution)/shard_map/ppermute | solution.py:25
  119.5 23.7 %collective-permute-start.21 = (bf16[2,2,128,256]{3,2,0,1:T(8,128)(2,1)}, bf16[2,2,128,256]{3,2,0,1:T(8,128)(2,1)}, u32[]{:S(2)}, u32[]{:S(2)}) collective-permute-start(bf16[2,2,128,256]{3,2,0,1:T(8,128)(2,1)} %get-tuple-element.131), channel_id=1, source_target_pairs={{0,2},{1,3},{2,0},{3,1},{4,6},{5,7},{6,4},{7,5},{8,10},{9,11},{10,... | collective-permute-start | bytes 786440 | tf_op jit(solution)/shard_map/ppermute | solution.py:25
  120.2 25.1 %collective-permute-start.20 = (bf16[2,2,128,256]{3,2,0,1:T(8,128)(2,1)}, bf16[2,2,128,256]{3,2,0,1:T(8,128)(2,1)}, u32[]{:S(2)}, u32[]{:S(2)}) collective-permute-start(bf16[2,2,128,256]{3,2,0,1:T(8,128)(2,1)} %get-tuple-element.131), channel_id=1, source_target_pairs={{0,3},{1,0},{2,1},{3,2},{4,7},{5,4},{6,5},{7,6},{8,11},{9,8},{10,9... | collective-permute-start | bytes 786440 | tf_op jit(solution)/shard_map/ppermute | solution.py:25
  126.3 22.7 %collective-permute-start.32 = (bf16[4,2,128,256]{3,2,1,0:T(8,128)(2,1)S(1)}, bf16[4,2,128,256]{3,2,1,0:T(8,128)(2,1)}, u32[]{:S(2)}, u32[]{:S(2)}) collective-permute-start(bf16[4,2,128,256]{3,2,1,0:T(8,128)(2,1)S(1)} %get-tuple-element.98), channel_id=1, source_target_pairs={{0,3},{1,0},{2,1},{3,2},{4,7},{5,4},{6,5},{7,6},{8,11},{9,8},{10,9... | collective-permute-start | bytes 1572872 | tf_op jit(solution)/shard_map/ppermute | solution.py:25
  143.2 25.2 %collective-permute-start.33 = (bf16[4,2,128,256]{3,2,1,0:T(8,128)(2,1)S(1)}, bf16[4,2,128,256]{3,2,1,0:T(8,128)(2,1)S(1)}, u32[]{:S(2)}, u32[]{:S(2)}) collective-permute-start(bf16[4,2,128,256]{3,2,1,0:T(8,128)(2,1)S(1)} %get-tuple-element.100), channel_id=1, source_target_pairs={{0,2},{1,3},{2,0},{3,1},{4,6},{5,7},{6,4},{7,5},{8,10},{9,11},{10,... | collective-permute-start | bytes 1572872 | tf_op jit(solution)/shard_map/ppermute | solution.py:25
  146.7 24.3 %collective-permute-start.23 = (bf16[4,2,128,256]{3,2,1,0:T(8,128)(2,1)S(1)}, bf16[4,2,128,256]{3,2,1,0:T(8,128)(2,1)S(1)}, u32[]{:S(2)}, u32[]{:S(2)}) collective-permute-start(bf16[4,2,128,256]{3,2,1,0:T(8,128)(2,1)S(1)} %get-tuple-element.101), channel_id=1, source_target_pairs={{0,12},{4,0},{8,4},{12,8},{1,13},{5,1},{9,5},{13,9},{2,14},{6,2},{... | collective-permute-start | bytes 1572872 | tf_op jit(solution)/shard_map/ppermute | solution.py:25
  148.1 23.0 %collective-permute-start.25 = (bf16[4,2,128,256]{3,2,1,0:T(8,128)(2,1)S(1)}, bf16[4,2,128,256]{3,2,1,0:T(8,128)(2,1)S(1)}, u32[]{:S(2)}, u32[]{:S(2)}) collective-permute-start(bf16[4,2,128,256]{3,2,1,0:T(8,128)(2,1)S(1)} %get-tuple-element.102), channel_id=1, source_target_pairs={{0,4},{4,8},{8,12},{12,0},{1,5},{5,9},{9,13},{13,1},{2,6},{6,10},{... | collective-permute-start | bytes 1572872 | tf_op jit(solution)/shard_map/ppermute | solution.py:25
  149.0 24.5 %collective-permute-start.24 = (bf16[4,2,128,256]{3,2,1,0:T(8,128)(2,1)S(1)}, bf16[4,2,128,256]{3,2,1,0:T(8,128)(2,1)S(1)}, u32[]{:S(2)}, u32[]{:S(2)}) collective-permute-start(bf16[4,2,128,256]{3,2,1,0:T(8,128)(2,1)S(1)} %get-tuple-element.103), channel_id=1, source_target_pairs={{0,8},{4,12},{8,0},{12,4},{1,9},{5,13},{9,1},{13,5},{2,10},{6,14},... | collective-permute-start | bytes 1572872 | tf_op jit(solution)/shard_map/ppermute | solution.py:25
  187.1 30.0 %collective-permute-start.43 = (bf16[4,2,128,256]{3,2,1,0:T(8,128)(2,1)S(1)}, bf16[4,2,128,256]{3,2,1,0:T(8,128)(2,1)S(1)}, u32[]{:S(2)}, u32[]{:S(2)}) collective-permute-start(bf16[4,2,128,256]{3,2,1,0:T(8,128)(2,1)S(1)} %bitcast.313), channel_id=1, source_target_pairs={{0,3},{1,0},{2,1},{3,2},{4,7},{5,4},{6,5},{7,6},{8,11},{9,8},{10,9... | collective-permute-start | bytes 1572872 | tf_op jit(solution)/shard_map/ppermute | solution.py:29
  190.0 29.4 %collective-permute-start.41 = (bf16[4,2,128,256]{3,2,1,0:T(8,128)(2,1)S(1)}, bf16[4,2,128,256]{3,2,1,0:T(8,128)(2,1)S(1)}, u32[]{:S(2)}, u32[]{:S(2)}) collective-permute-start(bf16[4,2,128,256]{3,2,1,0:T(8,128)(2,1)S(1)} %bitcast.311), channel_id=1, source_target_pairs={{0,1},{1,2},{2,3},{3,0},{4,5},{5,6},{6,7},{7,4},{8,9},{9,10},{10,1... | collective-permute-start | bytes 1572872 | tf_op jit(solution)/shard_map/ppermute | solution.py:29
  193.2 22.5 %collective-permute-start.54 = (bf16[4,2,128,256]{3,2,1,0:T(8,128)(2,1)S(1)}, bf16[4,2,128,256]{3,2,1,0:T(8,128)(2,1)S(1)}, u32[]{:S(2)}, u32[]{:S(2)}) collective-permute-start(bf16[4,2,128,256]{3,2,1,0:T(8,128)(2,1)S(1)} %bitcast.314), channel_id=1, source_target_pairs={{0,4},{4,8},{8,12},{12,0},{1,5},{5,9},{9,13},{13,1},{2,6},{6,10},{... | collective-permute-start | bytes 1572872 | tf_op jit(solution)/shard_map/ppermute | solution.py:29
  206.8 28.1 %collective-permute-start.49 = (bf16[4,2,128,256]{3,2,1,0:T(8,128)(2,1)S(1)}, bf16[4,2,128,256]{3,2,1,0:T(8,128)(2,1)S(1)}, u32[]{:S(2)}, u32[]{:S(2)}) collective-permute-start(bf16[4,2,128,256]{3,2,1,0:T(8,128)(2,1)S(1)} %bitcast.312), channel_id=1, source_target_pairs={{0,12},{4,0},{8,4},{12,8},{1,13},{5,1},{9,5},{13,9},{2,14},{6,2},{... | collective-permute-start | bytes 1572872 | tf_op jit(solution)/shard_map/ppermute | solution.py:29
  215.7 22.2 %collective-permute-start.47 = (bf16[4,2,128,256]{3,2,1,0:T(8,128)(2,1)S(1)}, bf16[4,2,128,256]{3,2,1,0:T(8,128)(2,1)S(1)}, u32[]{:S(2)}, u32[]{:S(2)}) collective-permute-start(bf16[4,2,128,256]{3,2,1,0:T(8,128)(2,1)S(1)} %bitcast.310), channel_id=1, source_target_pairs={{0,4},{4,8},{8,12},{12,0},{1,5},{5,9},{9,13},{13,1},{2,6},{6,10},{... | collective-permute-start | bytes 1572872 | tf_op jit(solution)/shard_map/ppermute | solution.py:29
  217.2 22.4 %collective-permute-start.48 = (bf16[4,2,128,256]{3,2,1,0:T(8,128)(2,1)S(1)}, bf16[4,2,128,256]{3,2,1,0:T(8,128)(2,1)S(1)}, u32[]{:S(2)}, u32[]{:S(2)}) collective-permute-start(bf16[4,2,128,256]{3,2,1,0:T(8,128)(2,1)S(1)} %bitcast.308), channel_id=1, source_target_pairs={{0,8},{4,12},{8,0},{12,4},{1,9},{5,13},{9,1},{13,5},{2,10},{6,14},... | collective-permute-start | bytes 1572872 | tf_op jit(solution)/shard_map/ppermute | solution.py:29
  219.3 131.1 %collective-permute-start.35 = (bf16[4,448,512]{2,1,0:T(8,128)(2,1)S(1)}, bf16[4,448,512]{2,1,0:T(8,128)(2,1)S(1)}, u32[]{:S(2)}, u32[]{:S(2)}) collective-permute-start(bf16[4,448,512]{2,1,0:T(8,128)(2,1)S(1)} %slice.489), channel_id=1, source_target_pairs={{0,32},{32,0},{1,33},{33,1},{2,34},{34,2},{3,35},{35,3},{4,36},{36... | collective-permute-start | bytes 5505032 | tf_op jit(solution)/shard_map/ppermute | solution.py:34
  219.3 160.8 %collective-permute-start.38 = (bf16[4,448,512]{2,1,0:T(8,128)(2,1)S(1)}, bf16[4,448,512]{2,1,0:T(8,128)(2,1)S(1)}, u32[]{:S(2)}, u32[]{:S(2)}) collective-permute-start(bf16[4,448,512]{2,1,0:T(8,128)(2,1)S(1)} %slice.495), channel_id=1, source_target_pairs={{0,32},{32,0},{1,33},{33,1},{2,34},{34,2},{3,35},{35,3},{4,36},{36... | collective-permute-start | bytes 5505032 | tf_op jit(solution)/shard_map/ppermute | solution.py:34
  308.1 25.4 %collective-permute-start.68 = (bf16[4,2,128,256]{3,2,1,0:T(8,128)(2,1)S(1)}, bf16[4,2,128,256]{3,2,1,0:T(8,128)(2,1)S(1)}, u32[]{:S(2)}, u32[]{:S(2)}) collective-permute-start(bf16[4,2,128,256]{3,2,1,0:T(8,128)(2,1)S(1)} %bitcast.325), channel_id=1, source_target_pairs={{0,3},{1,0},{2,1},{3,2},{4,7},{5,4},{6,5},{7,6},{8,11},{9,8},{10,9... | collective-permute-start | bytes 1572872 | tf_op jit(solution)/shard_map/ppermute | solution.py:29
  317.1 20.0 %collective-permute-start.67 = (bf16[4,2,128,256]{3,2,1,0:T(8,128)(2,1)S(1)}, bf16[4,2,128,256]{3,2,1,0:T(8,128)(2,1)S(1)}, u32[]{:S(2)}, u32[]{:S(2)}) collective-permute-start(bf16[4,2,128,256]{3,2,1,0:T(8,128)(2,1)S(1)} %bitcast.318), channel_id=1, source_target_pairs={{0,2},{1,3},{2,0},{3,1},{4,6},{5,7},{6,4},{7,5},{8,10},{9,11},{10,... | collective-permute-start | bytes 1572872 | tf_op jit(solution)/shard_map/ppermute | solution.py:29
  351.0 54.6 %collective-permute-start.36 = (bf16[2,448,512]{2,1,0:T(8,128)(2,1)S(1)}, bf16[2,448,512]{2,1,0:T(8,128)(2,1)}, u32[]{:S(2)}, u32[]{:S(2)}) collective-permute-start(bf16[2,448,512]{2,1,0:T(8,128)(2,1)S(1)} %slice.491), channel_id=1, source_target_pairs={{0,64},{64,0},{128,192},{192,128},{1,65},{65,1},{129,193},{193,129... | collective-permute-start | bytes 2752520 | tf_op jit(solution)/shard_map/ppermute | solution.py:34
  376.7 28.8 %collective-permute-start.78 = (bf16[2,128,256]{2,1,0:T(8,128)(2,1)S(1)}, bf16[2,128,256]{2,1,0:T(8,128)(2,1)S(1)}, u32[]{:S(2)}, u32[]{:S(2)}) collective-permute-start(bf16[2,128,256]{2,1,0:T(8,128)(2,1)S(1)} %pad_maximum_fusion.17), channel_id=1, source_target_pairs={{0,16},{16,0},{1,17},{17,1},{2,18},{18,2},{3,19},{19,3},{4,20},{20... | collective-permute-start | bytes 393224 | tf_op jit(solution)/shard_map/ppermute | solution.py:34
  382.9 35.9 %collective-permute-start.39 = (bf16[2,448,512]{2,1,0:T(8,128)(2,1)}, bf16[2,448,512]{2,1,0:T(8,128)(2,1)}, u32[]{:S(2)}, u32[]{:S(2)}) collective-permute-start(bf16[2,448,512]{2,1,0:T(8,128)(2,1)} %slice.497), channel_id=1, source_target_pairs={{0,64},{64,0},{128,192},{192,128},{1,65},{65,1},{129,193},{193,129... | collective-permute-start | bytes 2752520 | tf_op jit(solution)/shard_map/ppermute | solution.py:34
  407.1 35.6 %collective-permute-start.37 = (bf16[448,512]{1,0:T(8,128)(2,1)S(1)}, bf16[448,512]{1,0:T(8,128)(2,1)S(1)}, u32[]{:S(2)}, u32[]{:S(2)}) collective-permute-start(bf16[448,512]{1,0:T(8,128)(2,1)S(1)} %slice_bitcast_fusion.4), channel_id=1, source_target_pairs={{0,128},{64,192},{128,0},{192,64},{1,129},{65,193},{129,1},{193,65... | collective-permute-start | bytes 1376264 | tf_op jit(solution)/shard_map/ppermute | solution.py:34
  420.2 28.5 %collective-permute-start.40 = (bf16[448,512]{1,0:T(8,128)(2,1)S(1)}, bf16[448,512]{1,0:T(8,128)(2,1)S(1)}, u32[]{:S(2)}, u32[]{:S(2)}) collective-permute-start(bf16[448,512]{1,0:T(8,128)(2,1)S(1)} %slice_bitcast_fusion.2), channel_id=1, source_target_pairs={{0,128},{64,192},{128,0},{192,64},{1,129},{65,193},{129,1},{193,65... | collective-permute-start | bytes 1376264 | tf_op jit(solution)/shard_map/ppermute | solution.py:34
  (61 other events, 680.2 us)
